TPU v7x, 256 devices: a whole 4x4x8 slice. The times are simulated.
256 devices in a mesh: dp: 4 (over x), vocab: 64 (over y, z, core).
Axes of the slice: x: 4, y: 4, z: 8, core: 2. Of those that a mesh axis runs over, the one named last changes fastest.
Arguments:
- features: bfloat16 [2048, 4096], P(('dp', 'vocab')), may hold values from -8 to 8
- head: bfloat16 [65536, 4096], P(('dp', 'vocab')), may hold values from -0.5 to 0.5
- momentum: bfloat16 [65536, 4096], P(('dp', 'vocab')), may hold values from -7.124618e-08 to 7.124618e-08
- hessian: bfloat16 [65536, 4096], P(('dp', 'vocab')), may hold values from 4.765752e-10 to 4.7683716e-06
- true_labels: int32 [2048], replicated, may hold values from 0 to 65535
- sampled_labels: int32 [2048], replicated, may hold values from 0 to 65535
Outputs:
- mean_loss: float32 [], replicated
- new_hessian: bfloat16 [65536, 4096], P(('dp', 'vocab'))
- update: bfloat16 [65536, 4096], P(('dp', 'vocab'))
All inputs are finite; a program needn't handle non-finite values.
Results may differ from a plain program's by a relative error of at most 0.019.
Values may be sent and summed in bfloat16 or wider, within the bound.
A program may use at most 128 MiB of HBM per device.

v0:
```python
import jax
import jax.numpy as jnp
from jax import lax
from jax.sharding import PartitionSpec as P

hess_decay = 0.99
clip_scale = 0.05


def local_stats(logits, columns, labels):
    highest = jnp.max(logits, axis=1)
    row_total = jnp.sum(jnp.exp(logits - highest[:, None]), axis=1)
    picked = jnp.sum(jnp.where(columns[None, :] == labels[:, None], logits, 0.0), axis=1)
    return (highest, row_total, picked)


def make_signal(logits, log_norm, columns, labels):
    chosen = (columns[None, :] == labels[:, None]).astype(jnp.float32)
    return (jnp.exp(logits - log_norm[:, None]) - chosen).astype(jnp.bfloat16)


def sophia_tail(gradient, momentum, hessian):
    fresh = hess_decay * hessian.astype(jnp.float32) + (1.0 - hess_decay) * gradient * gradient
    clipped = jnp.clip(momentum.astype(jnp.float32) / (clip_scale * fresh), -1.0, 1.0)
    return (fresh.astype(jnp.bfloat16), clipped.astype(jnp.bfloat16))


def shards(features, head, momentum, hessian, true_labels, sampled_labels):
    voc_dev = head.shape[0]
    every_row = lax.all_gather(features, ("dp", "vocab"), axis=0, tiled=True)
    logits = lax.dot_general(
        every_row, head, (((1,), (1,)), ((), ())), preferred_element_type=jnp.float32
    )
    own_offset = (lax.axis_index("dp") * lax.axis_size("vocab") + lax.axis_index("vocab")) * voc_dev
    columns = own_offset + jnp.arange(voc_dev, dtype=jnp.int32)
    highest, row_total, picked = local_stats(logits, columns, true_labels)
    top_all = lax.pmax(highest, ("dp", "vocab"))
    row_total, picked = lax.psum((row_total * jnp.exp(highest - top_all), picked), ("dp", "vocab"))
    highest = top_all
    log_norm = highest + jnp.log(row_total)
    mean_loss = jnp.mean(log_norm - picked)
    signal = make_signal(logits, log_norm, columns, sampled_labels)
    groups = lax.axis_size("dp")
    signal_groups = signal.reshape(groups, -1, voc_dev)
    row_groups = every_row.reshape(groups, -1, every_row.shape[1])
    partials = lax.dot_general(
        signal_groups, row_groups, (((1,), (1,)), ((0,), (0,))), preferred_element_type=jnp.float32
    )
    rounded = lax.optimization_barrier(partials.astype(jnp.bfloat16)).astype(jnp.float32)
    gradient = jnp.sum(rounded, axis=0)
    fresh, clipped = sophia_tail(gradient, momentum, hessian)
    return (mean_loss, fresh, clipped)


def solution(mesh):
    in_specs = (
        P(("dp", "vocab"), None),
        P(("dp", "vocab"), None),
        P(("dp", "vocab"), None),
        P(("dp", "vocab"), None),
        P(),
        P(),
    )
    out_specs = (P(), P(("dp", "vocab"), None), P(("dp", "vocab"), None))
    return jax.shard_map(shards, mesh=mesh, in_specs=in_specs, out_specs=out_specs, check_vma=False)
```

profile of v0, /device:TPU:1, one launch (start us, length us, event | category | flops | bytes accessed | tf_op | source)
XLA Modules:
  0.0 339.7 jit_solution(14028145733843676023)
XLA Ops:
  7.2 0.0 copy-start
  7.2 0.0 all-gather.2.cloned.1.call-start
  7.2 0.7 all-gather.2.cloned.1.call-update
  7.9 0.0 copy-start.1
  7.9 133.0 %all-gather.2.cloned.1.call-done = bf16[2048,4096]{1,0:T(8,128)(2,1)} async-done(((bf16[8,4096]{1,0:T(8,128)(2,1)}), bf16[2048,4096]{1,0:T(8,128)(2,1)}) %all-gather.2.cloned.1.call-update) | async-done | bytes 16777232 | tf_op jit(solution)/shard_map/all_gather | solution.py:30
  140.9 0.0 copy-done
  140.9 9.8 %fusion.2 = (f32[2048]{0:T(1024)S(1)}, f32[2048,256]{1,0:T(8,128)}) fusion(bf16[2048,4096]{1,0:T(8,128)(2,1)} %all-gather.2.cloned.1.call-done, bf16[256,4096]{1,0:T(8,128)(2,1)S(1)} %copy-done), kind=kOutput, calls=%fused_computation.13 | convolution fusion | flops 4295489536 | bytes 20979712 | tf_op jit(solution)/shard_map/dot_general | solution.py:31
  150.8 0.0 copy-start.2
  150.8 74.4 %pmax.7 = f32[2048]{0:T(1024)S(1)} all-reduce(f32[2048]{0:T(1024)S(1)} %get-tuple-element.11), channel_id=1, replica_groups=mesh['dp'=4,'vocab'=64] {'dp','vocab'}, use_global_device_ids=true, to_apply=%region_1.0 | all-reduce | flops 2048 | bytes 16384 | tf_op jit(solution)/shard_map/pmax | solution.py:37
  225.2 0.0 copy-done.1
  225.2 2.5 select_reduce_fusion
  227.7 73.8 %all-reduce = (f32[2048]{0:T(1024)S(1)}, f32[2048]{0:T(1024)S(1)}) all-reduce(f32[2048]{0:T(1024)S(1)} %exponential_multiply_fusion, f32[2048]{0:T(1024)S(1)} %get-tuple-element.3), channel_id=1, replica_groups=mesh['dp'=4,'vocab'=64] {'dp','vocab'}, use_global_device_ids=true, to_apply=%region_3.4 | all-reduce | flops 4096 | bytes 32768 | tf_op jit(solution)/shard_map/psum | solution.py:38
  301.5 0.6 subtract_reduce_fusion
  302.1 0.0 copy-done.2
  302.2 1.9 subtract_convert_fusion
  304.1 12.6 %convolution_convert_fusion = bf16[4,256,4096]{2,1,0:T(8,128)(2,1)} fusion(bf16[4,512,256]{2,1,0:T(8,128)(2,1)S(1)} %bitcast.7, bf16[4,512,4096]{2,1,0:T(8,128)(2,1)} %bitcast.6), kind=kOutput, calls=%fused_computation.1 | convolution fusion | flops 4299161600 | bytes 26214400 | tf_op jit(solution)/shard_map/dot_general | solution.py:46
  316.7 7.3 %convert_reduce_fusion = f32[256,4096]{1,0:T(8,128)} fusion(bf16[4,256,4096]{2,1,0:T(8,128)(2,1)} %convolution_convert_fusion), kind=kLoop, calls=%fused_computation | loop fusion | flops 7340032 | bytes 12582912 | tf_op jit(solution)/shard_map/reduce_sum | solution.py:50
  324.6 7.1 %clamp_convert_fusion = (bf16[256,4096]{1,0:T(8,128)(2,1)}, bf16[256,4096]{1,0:T(8,128)(2,1)}) fusion(bf16[256,4096]{1,0:T(8,128)(2,1)} %param.8, f32[256,4096]{1,0:T(8,128)} %convert_reduce_fusion, bf16[256,4096]{1,0:T(8,128)(2,1)} %param.9), kind=kLoop, calls=%fused_computation.4 | loop fusion | flops 11534336 | bytes 12582912 | tf_op jit(solution)/shard_map/convert_element_type | solution.py:25
  (2 shorter events, 0.0 us)
Async XLA Ops:
  7.2 133.7 %copy-start = (bf16[256,4096]{1,0:T(8,128)(2,1)S(1)}, bf16[256,4096]{1,0:T(8,128)(2,1)}, u32[]{:S(2)}) copy-start(bf16[256,4096]{1,0:T(8,128)(2,1)} %param.7) | copy-start | bytes 6291460
  7.2 133.7 %all-gather.2.cloned.1.call-start = ((), (), s32[]{:S(2)}) async-start(), calls=%async_computation | async-start | bytes 16842752 | tf_op jit(solution)/shard_map/all_gather | solution.py:30
  7.9 217.3 %copy-start.1 = (s32[2048]{0:T(1024)S(1)}, s32[2048]{0:T(1024)}, u32[]{:S(2)}) copy-start(s32[2048]{0:T(1024)} %param.10) | copy-start | bytes 24580
  150.8 151.4 %copy-start.2 = (s32[2048]{0:T(1024)S(1)}, s32[2048]{0:T(1024)}, u32[]{:S(2)}) copy-start(s32[2048]{0:T(1024)} %param.11) | copy-start | bytes 24580
Sparse Core Ops, SparseCore 0:
  11.7 129.1 all-gather.1
where the time goes:
time: 340 us
  blocking collectives  148 us (44%)
  waiting for transfers between devices  134 us (39%)
  matrix products  22.5 us (7%)
  other arithmetic  19.5 us (6%)
  between operations  15.9 us (5%)
    all_gather x1, waiting for transfers between devices, shards(): every_row = lax.all_gather(features, ('dp', 'vocab'), axis=0, tiled=True)  133 us
    pmax x1, blocking collectives, shards(): top_all = lax.pmax(highest, ('dp', 'vocab'))  74.4 us
    psum x1, blocking collectives, shards(): lax.psum((row_total * jnp.exp(highest - top_all), picked), ('dp', 'vocab'))  73.8 us
    dot_general x1, matrix products, shards(): lax.dot_general(signal_groups, row_groups, (((1,), (1,)), ((0,), (0,))),...  12.6 us
    dot_general x1, matrix products, shards(): lax.dot_general(every_row, head, (((1,), (1,)), ((), ())), preferred_elem...  9.85 us
    reduce_sum x1, other arithmetic, shards(): gradient = jnp.sum(rounded, axis=0)  7.29 us
    convert_element_type x1, other arithmetic, sophia_tail(): return (fresh.astype(jnp.bfloat16), clipped.astype(jnp.bfloat16))  7.12 us
  transfers between devices with their start and end apart: 1, of which 1 were waited for; matrix products, arithmetic and copies ran while one was open for 0% of the time, Pallas kernels for 0%

commit v1 on v0

v1 whole, which is shorter than its diff:
```python
import jax
import jax.numpy as jnp
from jax import lax
from jax.experimental import pallas as pl
from jax.experimental.pallas import tpu as pltpu
from jax.sharding import PartitionSpec as P

MESH = pl.DeviceIdType.MESH
hess_decay = 0.99
clip_scale = 0.05

NX, NY, NZ = 4, 4, 8
D = 4096
HALF = D // 2
ROWS = 16
BLOCK = 256
TOKENS = 2048
VOC = 256
STAT = 384


def gather_kernel(feat_ref, head_ref, true_ref, samp_ref,
                  feats_out, signal_ref, loss_ref,
                  pair, held, logits, stats_a, stats_b,
                  pair_s, pair_r, q_s, q_r, z_s, z_r, zh_s, zh_r,
                  p_s, p_r, s_s, s_r, a_s, a_r, b_s, b_r, out_sem):
    x = lax.axis_index("dp")
    v = lax.axis_index("vocab")
    y, z, c = v // 16, (v // 2) % 8, v % 2
    p = jnp.where(c == 0, x, y)
    q = jnp.where(c == 0, y, x)

    def device(px, qx, zx):
        xx = jnp.where(c == 0, px, qx)
        yy = jnp.where(c == 0, qx, px)
        return (xx, yy * 16 + zx * 2 + c)

    sister = (x, y * 16 + z * 2 + 1 - c)
    p_up, p_dn = (p + 1) % 4, (p + 3) % 4
    q_up, q_dn = (q + 1) % 4, (q + 3) % 4
    z_up, z_dn = (z + 1) % 8, (z + 7) % 8

    def remote(src, dst, ssem, rsem, dev):
        return pltpu.make_async_remote_copy(src, dst, ssem, rsem, device_id=dev, device_id_type=MESH)

    barrier = pltpu.get_barrier_semaphore()
    for dev in (sister, device(p_up, q, z), device(p_dn, q, z), device(p, q_up, z), device(p, q_dn, z),
                device(p, q, z_up), device(p, q, z_dn)):
        pl.semaphore_signal(barrier, inc=1, device_id=dev, device_id_type=MESH)
    pl.semaphore_wait(barrier, 7)

    theirs = pl.multiple_of((1 - c) * HALF, HALF)
    mine = pl.multiple_of(c * HALF, HALF)
    pair_copy = remote(feat_ref.at[:, pl.ds(theirs, HALF)], pair.at[c], pair_s, pair_r, sister)
    pair_copy.start()
    pair[c] = feat_ref[:, pl.ds(mine, HALF)]
    pair_copy.wait_recv()
    held[c, z, p, q] = pair[...].reshape(ROWS, HALF)

    def slab(qx):
        return held.at[c, z, p, qx]

    q_copies = [
        remote(slab(q), slab(q), q_s.at[0], q_r.at[0], device(p, q_up, z)),
        remote(slab(q), slab(q), q_s.at[1], q_r.at[1], device(p, q_dn, z)),
        remote(slab(q_dn), slab(q_dn), q_s.at[2], q_r.at[2], device(p, q_up, z)),
    ]
    q_copies[0].start()
    q_copies[1].start()
    q_copies[0].wait_recv()
    q_copies[2].start()
    q_copies[1].wait_recv()
    q_copies[2].wait_recv()

    def plane(s):
        off = jnp.where(s % 2 == 1, 8 - (s + 1) // 2, s // 2)
        return (z + off) % 8

    def chunk(zx, px):
        return held.at[c, zx, px]

    def part(zx, px, half):
        return held.at[c, zx, px, pl.ds(half * 2, 2)]

    def z_copy(s):
        zx = plane(s)
        to = jnp.where(s % 2 == 1, z_up, z_dn)
        return remote(chunk(zx, p), chunk(zx, p), z_s.at[s + 2], z_r.at[s + 2], device(p, q, to))

    def z_half(s):
        zx = plane(s)
        to = jnp.where(s % 2 == 1, z_up, z_dn)
        return remote(part(zx, p, s - 5), part(zx, p, s - 5), zh_s.at[s - 5], zh_r.at[s - 5], device(p, q, to))

    def z_first():
        return remote(chunk(z, p), chunk(z, p), z_s.at[1], z_r.at[1], device(p, q, z_up))

    def p_copies(s):
        zx = plane(s)
        return (remote(chunk(zx, p), chunk(zx, p), p_s.at[s, 0], p_r.at[s, 0], device(p_up, q, z)),
                remote(chunk(zx, p), chunk(zx, p), p_s.at[s, 1], p_r.at[s, 1], device(p_dn, q, z)))

    def p_halves(s):
        zx = plane(s)
        return (remote(part(zx, p_dn, 0), part(zx, p_dn, 0), p_s.at[s, 2], p_r.at[s, 2], device(p_up, q, z)),
                remote(part(zx, p_up, 1), part(zx, p_up, 1), p_s.at[s, 3], p_r.at[s, 3], device(p_dn, q, z)))

    def s_copy(s, which, px):
        zx = plane(s)
        return remote(chunk(zx, px), chunk(zx, px), s_s.at[s, which], s_r.at[s, which], sister)

    p_far = (p + 2) % 4

    def spread(s):
        for copy in p_copies(s):
            copy.start()
        s_copy(s, 0, p).start()

    z_first().start()
    z_copy(0).start()
    spread(0)

    own_offset = (x * 64 + v) * VOC
    rows = own_offset + lax.broadcasted_iota(jnp.int32, (VOC, BLOCK), 0)
    lanes = lax.broadcasted_iota(jnp.int32, (1, STAT), 1)
    planes = lax.broadcasted_iota(jnp.int32, (NZ, STAT), 0)
    stats_a[x * 4 + y] = jnp.zeros((NZ, STAT), jnp.float32)

    def out_copies(s):
        zx = plane(s)
        copies = [pltpu.make_async_copy(held.at[0, zx], feats_out.at[zx, :, :, :, pl.ds(0, HALF)], out_sem.at[s, 0])]
        for yy in range(NY):
            copies.append(pltpu.make_async_copy(
                held.at[1, zx, yy], feats_out.at[zx, :, yy, :, pl.ds(HALF, HALF)], out_sem.at[s, 1 + yy]))
        return copies

    def compute(s):
        zx = plane(s)
        left = held[0, zx].reshape(BLOCK, HALF)
        total = lax.dot_general(head_ref[:, :HALF], left, (((1,), (1,)), ((), ())), preferred_element_type=jnp.float32)
        right = jnp.concatenate([held[1, zx, yy, xx] for xx in range(NX) for yy in range(NY)], axis=0)
        total += lax.dot_general(head_ref[:, HALF:], right, (((1,), (1,)), ((), ())), preferred_element_type=jnp.float32)
        logits[zx] = total
        highest = jnp.max(total, axis=0, keepdims=True)
        lse = highest + jnp.log(jnp.sum(jnp.exp(total - highest), axis=0, keepdims=True))
        labels = true_ref[pl.ds(zx, 1), :]
        picked = jnp.sum(jnp.where(rows == labels, total, 0.0), axis=0, keepdims=True)
        return zx, lse, picked

    me_xy = x * 4 + y
    me_zc = z * 2 + c

    def step(i, carry):
        @pl.when(jnp.logical_and(i >= 1, i <= 6))
        def _():
            z_copy(i - 2).wait_recv()

        @pl.when(jnp.logical_and(i >= 1, i <= 4))
        def _():
            z_copy(i).start()

        @pl.when(jnp.logical_or(i == 5, i == 6))
        def _():
            z_half(i).start()

        @pl.when(i == 7)
        def _():
            z_half(5).wait_recv()
            z_half(6).wait_recv()

        @pl.when(jnp.logical_and(i >= 1, i <= 7))
        def _():
            spread(i)

        @pl.when(jnp.logical_and(i >= 1, i <= 8))
        def _():
            s = i - 1
            first, second = p_copies(s)
            on, back = p_halves(s)
            first.wait_recv()
            on.start()
            s_copy(s, 1, p_dn).start()
            second.wait_recv()
            back.start()
            s_copy(s, 2, p_up).start()

        @pl.when(jnp.logical_and(i >= 2, i <= 9))
        def _():
            s = i - 2
            on, back = p_halves(s)
            on.wait_recv()
            back.wait_recv()
            s_copy(s, 3, p_far).start()

        @pl.when(i >= 3)
        def _():
            s = i - 3
            for which in range(4):
                s_copy(s, which, p).wait_recv()
            for copy in out_copies(s):
                copy.start()
            zx, lse, picked = compute(s)
            fresh_row = jnp.concatenate([lse, picked[:, :128] + picked[:, 128:]], axis=1)
            stats_a[me_xy] = jnp.where(planes == zx, fresh_row, stats_a[me_xy])

        return carry

    lax.fori_loop(0, 11, step, 0)

    def a_copy(j):
        return remote(stats_a.at[me_xy], stats_a.at[me_xy], a_s.at[j], a_r.at[me_xy], (j // 4, (j % 4) * 16 + z * 2 + c))

    def a_arrival(j):
        return remote(stats_a.at[j], stats_a.at[j], a_s.at[j], a_r.at[j], (j // 4, (j % 4) * 16 + z * 2 + c))

    def b_copy(j):
        return remote(stats_b.at[me_zc], stats_b.at[me_zc], b_s.at[j], b_r.at[me_zc], (x, y * 16 + j))

    def b_arrival(j):
        return remote(stats_b.at[j], stats_b.at[j], b_s.at[j], b_r.at[j], (x, y * 16 + j))

    def each_other(me, action):
        def one(j, carry):
            @pl.when(j != me)
            def _():
                action(j)
            return carry
        lax.fori_loop(0, 16, one, 0)

    def combine(stats):
        values = [stats[j] for j in range(16)]
        top = values[0]
        for value in values[1:]:
            top = jnp.maximum(top, value)
        total = jnp.exp(values[0] - top)
        added = values[0]
        for value in values[1:]:
            total += jnp.exp(value - top)
            added += value
        return jnp.where(lanes < BLOCK, top + jnp.log(total), added)

    each_other(me_xy, lambda j: a_copy(j).start())
    each_other(me_xy, lambda j: a_arrival(j).wait_recv())
    stats_b[me_zc] = combine(stats_a)
    each_other(me_zc, lambda j: b_copy(j).start())
    each_other(me_zc, lambda j: b_arrival(j).wait_recv())
    final = combine(stats_b)
    signed = jnp.where(lanes < BLOCK, final, -final)
    loss_ref[...] = jnp.sum(jnp.sum(signed, axis=1, keepdims=True), axis=0, keepdims=True) * (1.0 / TOKENS)
    for zx in range(NZ):
        log_norm = final[zx:zx + 1, :BLOCK]
        chosen = (rows == samp_ref[zx:zx + 1, :]).astype(jnp.float32)
        signal_ref[:, zx * BLOCK:(zx + 1) * BLOCK] = (jnp.exp(logits[zx] - log_norm) - chosen).astype(jnp.bfloat16)

    pair_copy.wait_send()
    for copy in q_copies:
        copy.wait_send()
    z_first().wait_send()

    def finish(s, carry):
        @pl.when(s <= 4)
        def _():
            z_copy(s).wait_send()

        for copy in p_copies(s) + p_halves(s):
            copy.wait_send()
        for which in range(4):
            s_copy(s, which, p).wait_send()
        for copy in out_copies(s):
            copy.wait()
        return carry

    lax.fori_loop(0, 8, finish, 0)
    z_half(5).wait_send()
    z_half(6).wait_send()
    each_other(me_xy, lambda j: a_copy(j).wait_send())
    each_other(me_zc, lambda j: b_copy(j).wait_send())


def gather_call(features, head, true_labels, sampled_labels):
    dma = pltpu.SemaphoreType.DMA
    vmem = pl.BlockSpec(memory_space=pltpu.VMEM)
    return pl.pallas_call(
        gather_kernel,
        out_shape=(
            jax.ShapeDtypeStruct((NZ, NX, NY, ROWS, D), jnp.bfloat16),
            jax.ShapeDtypeStruct((VOC, TOKENS), jnp.bfloat16),
            jax.ShapeDtypeStruct((1, 1), jnp.float32),
        ),
        in_specs=[vmem] * 4,
        out_specs=(pl.BlockSpec(memory_space=pl.ANY), vmem, vmem),
        scratch_shapes=[
            pltpu.VMEM((2, 8, HALF), jnp.bfloat16),
            pltpu.VMEM((2, NZ, 4, 4, ROWS, HALF), jnp.bfloat16),
            pltpu.VMEM((NZ, VOC, BLOCK), jnp.float32),
            pltpu.VMEM((16, NZ, STAT), jnp.float32),
            pltpu.VMEM((16, NZ, STAT), jnp.float32),
            dma, dma, dma((3,)), dma((3,)), dma((8,)), dma((8,)), dma((2,)), dma((2,)),
            dma((8, 4)), dma((8, 4)), dma((8, 4)), dma((8, 4)),
            dma((16,)), dma((16,)), dma((16,)), dma((16,)), dma((8, 5)),
        ],
        compiler_params=pltpu.CompilerParams(collective_id=0, has_side_effects=True, vmem_limit_bytes=40 << 20),
        name="gather_logits",
    )(features, head, true_labels, sampled_labels)


def update_kernel(signal_ref, feats_ref, momentum_ref, hessian_ref, fresh_ref, clipped_ref):
    gradient = jnp.dot(signal_ref[...], feats_ref[...], preferred_element_type=jnp.float32)
    fresh = hess_decay * hessian_ref[...].astype(jnp.float32) + (1.0 - hess_decay) * gradient * gradient
    fresh_ref[...] = fresh.astype(jnp.bfloat16)
    clipped = jnp.clip(momentum_ref[...].astype(jnp.float32) / (clip_scale * fresh), -1.0, 1.0)
    clipped_ref[...] = clipped.astype(jnp.bfloat16)


def update_call(signal, feats, momentum, hessian):
    width = 512
    tile = pl.BlockSpec((VOC, width), lambda j: (0, j))
    out = jax.ShapeDtypeStruct((VOC, D), jnp.bfloat16)
    return pl.pallas_call(
        update_kernel,
        grid=(D // width,),
        out_shape=(out, out),
        in_specs=[
            pl.BlockSpec((VOC, TOKENS), lambda j: (0, 0)),
            pl.BlockSpec((TOKENS, width), lambda j: (0, j)),
            tile,
            tile,
        ],
        out_specs=(tile, tile),
        compiler_params=pltpu.CompilerParams(vmem_limit_bytes=40 << 20),
        name="gradient_update",
    )(signal, feats, momentum, hessian)


def by_plane(labels):
    return labels.reshape(NX, NY, NZ, ROWS).transpose(2, 0, 1, 3).reshape(NZ, BLOCK)


def shards(features, head, momentum, hessian, true_labels, sampled_labels):
    feats, signal, loss = gather_call(features, head, by_plane(true_labels), by_plane(sampled_labels))
    fresh, clipped = update_call(signal, feats.reshape(TOKENS, D), momentum, hessian)
    return (loss.reshape(()), fresh, clipped)


def solution(mesh):
    rows = P(("dp", "vocab"), None)
    return jax.shard_map(
        shards,
        mesh=mesh,
        in_specs=(rows, rows, rows, rows, P(), P()),
        out_specs=(P(), rows, rows),
        check_vma=False,
    )
```

time: 340 us -> 97.5 us (0.29)
  blocking collectives: 148 us -> 0 us
  waiting for transfers between devices: 134 us -> 0 us
  Pallas kernels: 0 us -> 88.7 us
  matrix products: 22.5 us -> 0 us
  other arithmetic: 19.5 us -> 0 us
  between operations: 15.9 us -> 2.51 us
  local copies, waits for them, and re-layouts: 0.02 us -> 5.83 us
    all_gather x1 -> x0, waiting for transfers between devices: 133 us -> none  [shards(): every_row = lax.all_gather(features, ('dp', 'vocab'), axis=0, tiled=True)]
    pallas_call x0 -> x2, Pallas kernels: none -> 88.7 us  [the longest x1 76.3 us: gather_call(): pl.pallas_call(gather_kernel, out_shape=(jax.ShapeDtypeStruct((NZ, NX, NY...]
    pmax x1 -> x0, blocking collectives: 74.4 us -> none  [shards(): top_all = lax.pmax(highest, ('dp', 'vocab'))]
    psum x1 -> x0, blocking collectives: 73.8 us -> none  [shards(): lax.psum((row_total * jnp.exp(highest - top_all), picked), ('dp', 'vocab'))]
    dot_general x2 -> x0, matrix products: 22.5 us -> none  [the longest x1 12.6 us: shards(): lax.dot_general(signal_groups, row_groups, (((1,), (1,)), ((0,), (0,))),...]
    reduce_sum x3 -> x0, other arithmetic: 10.4 us -> none  [the longest x1 7.29 us: shards(): gradient = jnp.sum(rounded, axis=0)]
    convert_element_type x2 -> x0, other arithmetic: 9.05 us -> none  [the longest x1 7.12 us: sophia_tail(): return (fresh.astype(jnp.bfloat16), clipped.astype(jnp.bfloat16))]
    unnamed x6 -> x8, local copies, waits for them, and re-layouts: 0.02 us -> 4.02 us
  transfers between devices with their start and end apart: 1 -> 0, of which waited for: 1 -> 0; matrix products, arithmetic and copies ran while one was open for 0% -> 0% of each run, Pallas kernels for 0% -> 0%
where the time goes in v1:
time: 97.5 us; the launch traced here: 97 us
  Pallas kernels  88.7 us (91%)
  local copies, waits for them, and re-layouts  5.83 us (6%)
  between operations  2.51 us (3%)
    pallas_call x1, Pallas kernels, gather_call(): pl.pallas_call(gather_kernel, out_shape=(jax.ShapeDtypeStruct((NZ, NX, NY...  76.3 us
    pallas_call x1, Pallas kernels, update_call(): pl.pallas_call(update_kernel, grid=(D // width,), out_shape=(out, out), i...  12.4 us
    unnamed x8, local copies, waits for them, and re-layouts  4.02 us

profile of v1, /device:TPU:1, one launch (start us, length us, event | category | flops | bytes accessed | tf_op | source)
XLA Modules:
  0.0 97.0 jit_solution(8435076700088719255)
XLA Ops:
  0.6 0.8 reshape.24
  1.4 0.1 reshape.25.true_ref
  1.5 0.8 reshape.26
  2.4 0.1 reshape.27.samp_ref
  2.5 0.0 copy-start
  2.5 1.6 %copy-done = bf16[256,4096]{1,0:T(8,128)(2,1)S(1)} copy-done((bf16[256,4096]{1,0:T(8,128)(2,1)S(1)}, bf16[256,4096]{1,0:T(8,128)(2,1)}, u32[]{:S(2)}) %copy-start) | copy-done | bytes 2097176
  4.1 0.0 copy-start.3
  4.1 0.8 copy-done.3
  4.9 0.0 copy-start.1
  4.9 76.3 %gather_logits.1 = (bf16[8,4,4,16,4096]{4,3,2,1,0:T(8,128)(2,1)}, bf16[256,2048]{1,0:T(8,128)(2,1)S(1)}, f32[1,1]{1,0:T(1,128)}) custom-call(bf16[8,4096]{1,0:T(8,128)(2,1)S(1)} %copy-done.3, bf16[256,4096]{1,0:T(8,128)(2,1)S(1)} %copy-done, s32[8,256]{1,0:T(8,128)S(1)} %reshape.25.true_ref, s32[8,256]{1,0:T(8,128)S(1)} %reshape.27.samp_ref), custom_call_target="tpu_custom_call" | custom-call | tf_op jit(solution)/shard_map/gather_logits/pallas_call | solution.py:283
  81.2 0.0 copy-done.1
  81.2 0.0 copy-start.2
  81.2 1.6 %copy-done.2 = bf16[256,4096]{1,0:T(8,128)(2,1)S(1)} copy-done((bf16[256,4096]{1,0:T(8,128)(2,1)S(1)}, bf16[256,4096]{1,0:T(8,128)(2,1)}, u32[]{:S(2)}) %copy-start.2) | copy-done | bytes 2097176
  82.8 12.4 %gradient_update.1 = (bf16[256,4096]{1,0:T(8,128)(2,1)}, bf16[256,4096]{1,0:T(8,128)(2,1)}) custom-call(bf16[256,2048]{1,0:T(8,128)(2,1)S(1)} %get-tuple-element.9.signal_ref, bf16[2048,4096]{1,0:T(8,128)(2,1)} %bitcast.4, bf16[256,4096]{1,0:T(8,128)(2,1)S(1)} %copy-done.1, bf16[256,4096]{1,0:T(8,128)(2,1)S(1)} %copy-done.2), custom_call_target="tpu_custom_call" | custom-call | tf_op jit(solution)/shard_map/gradient_update/pallas_call | solution.py:319
  (2 shorter events, 0.0 us)
Async XLA Ops:
  2.5 1.6 %copy-start = (bf16[256,4096]{1,0:T(8,128)(2,1)S(1)}, bf16[256,4096]{1,0:T(8,128)(2,1)}, u32[]{:S(2)}) copy-start(bf16[256,4096]{1,0:T(8,128)(2,1)} %head_ref.1) | copy-start | bytes 6291460
  4.1 0.8 copy-start.3
  4.9 76.3 %copy-start.1 = (bf16[256,4096]{1,0:T(8,128)(2,1)S(1)}, bf16[256,4096]{1,0:T(8,128)(2,1)}, u32[]{:S(2)}) copy-start(bf16[256,4096]{1,0:T(8,128)(2,1)} %momentum_ref.1) | copy-start | bytes 6291460
  81.2 1.6 %copy-start.2 = (bf16[256,4096]{1,0:T(8,128)(2,1)S(1)}, bf16[256,4096]{1,0:T(8,128)(2,1)}, u32[]{:S(2)}) copy-start(bf16[256,4096]{1,0:T(8,128)(2,1)} %hessian_ref.1) | copy-start | bytes 6291460

commit v2 on v1

v2 whole, which is shorter than its diff:
```python
import jax
import jax.numpy as jnp
from jax import lax
from jax.experimental import pallas as pl
from jax.experimental.pallas import tpu as pltpu
from jax.sharding import PartitionSpec as P

MESH = pl.DeviceIdType.MESH
hess_decay = 0.99
clip_scale = 0.05

NX, NY, NZ = 4, 4, 8
D = 4096
HALF = D // 2
ROWS = 16
BLOCK = 256
TOKENS = 2048
VOC = 256
STAT = 384
LAG1, LAG2, LAG3 = 2, 4, 5


def permute_labels(raw_ref, true_ref, samp_ref):
    labels = jnp.concatenate([raw_ref[0], raw_ref[1]], axis=0)
    pieces = jnp.concatenate([labels >> 8, labels & 255], axis=0).astype(jnp.float32).astype(jnp.bfloat16)
    source = lax.broadcasted_iota(jnp.int32, (128, BLOCK), 0)
    lane = lax.broadcasted_iota(jnp.int32, (128, BLOCK), 1)
    chip = lax.broadcasted_iota(jnp.int32, (ROWS, BLOCK), 0)
    owner = lax.broadcasted_iota(jnp.int32, (ROWS, BLOCK), 1) >> 4
    for zx in range(NZ):
        pick = (source == zx * ROWS + (lane & 15)).astype(jnp.float32).astype(jnp.bfloat16)
        spread = jnp.dot(pieces, pick, preferred_element_type=jnp.float32)
        rows = [jnp.sum(jnp.where(chip == owner, spread[k * 16:(k + 1) * 16], 0.0), axis=0, keepdims=True) for k in range(4)]
        true_ref[zx:zx + 1, :] = (rows[0] * 256.0 + rows[2]).astype(jnp.int32)
        samp_ref[zx:zx + 1, :] = (rows[1] * 256.0 + rows[3]).astype(jnp.int32)


def gather_kernel(feat_ref, head_hbm, true_hbm, samp_hbm,
                  held, signal_ref, loss_ref,
                  pair, head_ref, raw_ref, true_ref, samp_ref, logits, stats_a, stats_b,
                  pair_s, pair_r, q_s, q_r, zf_s, zf_r, z_s, z_r, zh_s, zh_r,
                  pf_s, pf_r, p_s, p_r, s_s, s_r, a_s, a_r, b_s, b_r, own_sem, head_sem, raw_sem):
    x = lax.axis_index("dp")
    v = lax.axis_index("vocab")
    y, z, c = v // 16, (v // 2) % 8, v % 2
    p = jnp.where(c == 0, x, y)
    q = jnp.where(c == 0, y, x)

    def device(px, qx, zx):
        xx = jnp.where(c == 0, px, qx)
        yy = jnp.where(c == 0, qx, px)
        return (xx, yy * 16 + zx * 2 + c)

    sister = (x, y * 16 + z * 2 + 1 - c)
    p_up, p_dn, p_far = (p + 1) % 4, (p + 3) % 4, (p + 2) % 4
    q_up, q_dn, q_far = (q + 1) % 4, (q + 3) % 4, (q + 2) % 4
    z_up, z_dn = (z + 1) % 8, (z + 7) % 8

    def remote(src, dst, ssem, rsem, dev):
        return pltpu.make_async_remote_copy(src, dst, ssem, rsem, device_id=dev, device_id_type=MESH)

    raw_copies = [pltpu.make_async_copy(true_hbm, raw_ref.at[0], raw_sem.at[0]),
                  pltpu.make_async_copy(samp_hbm, raw_ref.at[1], raw_sem.at[1])]
    for copy in raw_copies:
        copy.start()
    head_copy = pltpu.make_async_copy(head_hbm, head_ref, head_sem)
    head_copy.start()
    own_copy = pltpu.make_async_copy(feat_ref.at[:, pl.ds(pl.multiple_of(c * HALF, HALF), HALF)], pair.at[c], own_sem)
    own_copy.start()
    barrier = pltpu.get_barrier_semaphore()
    for dev in (sister, device(p_up, q, z), device(p_dn, q, z), device(p, q_up, z), device(p, q_dn, z),
                device(p, q, z_up), device(p, q, z_dn)):
        pl.semaphore_signal(barrier, inc=1, device_id=dev, device_id_type=MESH)
    pl.semaphore_wait(barrier, 7)

    theirs = pl.multiple_of((1 - c) * HALF, HALF)
    pair_copy = remote(feat_ref.at[:, pl.ds(theirs, HALF)], pair.at[c], pair_s, pair_r, sister)
    pair_copy.start()
    own_copy.wait()
    pair_copy.wait_recv()
    held[c, z, p, q] = pair[...].reshape(ROWS, HALF)

    def slab(qx):
        return held.at[c, z, p, qx]

    q_copies = [
        remote(slab(q), slab(q), q_s.at[0], q_r.at[0], device(p, q_up, z)),
        remote(slab(q), slab(q), q_s.at[1], q_r.at[1], device(p, q_dn, z)),
        remote(slab(q_dn), slab(q_dn), q_s.at[2], q_r.at[2], device(p, q_up, z)),
    ]
    order = (q, q_dn, q_up, q_far)

    def early(r):
        piece = slab(order[r])
        return [remote(piece, piece, pf_s.at[0, r], pf_r.at[0, r], device(p_up, q, z)),
                remote(piece, piece, pf_s.at[1, r], pf_r.at[1, r], device(p_dn, q, z)),
                remote(piece, piece, zf_s.at[0, r], zf_r.at[0, r], device(p, q, z_up)),
                remote(piece, piece, zf_s.at[1, r], zf_r.at[1, r], device(p, q, z_dn))]

    def start_early(r):
        for copy in early(r):
            copy.start()

    def plane(s):
        off = jnp.where(s % 2 == 1, 8 - (s + 1) // 2, s // 2)
        return (z + off) % 8

    def chunk(zx, px):
        return held.at[c, zx, px]

    def part(zx, px, half):
        return held.at[c, zx, px, pl.ds(half * 2, 2)]

    def z_copy(s):
        zx = plane(s)
        to = jnp.where(s % 2 == 1, z_up, z_dn)
        return remote(chunk(zx, p), chunk(zx, p), z_s.at[s + 2], z_r.at[s + 2], device(p, q, to))

    def z_half(s):
        zx = plane(s)
        to = jnp.where(s % 2 == 1, z_up, z_dn)
        return remote(part(zx, p, s - 5), part(zx, p, s - 5), zh_s.at[s - 5], zh_r.at[s - 5], device(p, q, to))

    def p_copies(s):
        zx = plane(s)
        return (remote(chunk(zx, p), chunk(zx, p), p_s.at[s, 0], p_r.at[s, 0], device(p_up, q, z)),
                remote(chunk(zx, p), chunk(zx, p), p_s.at[s, 1], p_r.at[s, 1], device(p_dn, q, z)))

    def p_halves(s):
        zx = plane(s)
        return (remote(part(zx, p_dn, 0), part(zx, p_dn, 0), p_s.at[s, 2], p_r.at[s, 2], device(p_up, q, z)),
                remote(part(zx, p_up, 1), part(zx, p_up, 1), p_s.at[s, 3], p_r.at[s, 3], device(p_dn, q, z)))

    def s_copy(s, which, px):
        zx = plane(s)
        return remote(chunk(zx, px), chunk(zx, px), s_s.at[s, which], s_r.at[s, which], sister)

    q_copies[0].start()
    q_copies[1].start()
    start_early(0)
    q_copies[0].wait_recv()
    q_copies[2].start()
    start_early(1)
    q_copies[1].wait_recv()
    start_early(2)
    for copy in raw_copies:
        copy.wait()
    permute_labels(raw_ref, true_ref, samp_ref)
    q_copies[2].wait_recv()
    start_early(3)
    s_copy(0, 0, p).start()

    own_offset = (x * 64 + v) * VOC
    rows = own_offset + lax.broadcasted_iota(jnp.int32, (VOC, BLOCK), 0)
    lanes = lax.broadcasted_iota(jnp.int32, (1, STAT), 1)
    planes = lax.broadcasted_iota(jnp.int32, (NZ, STAT), 0)
    me_xy = x * 4 + y
    me_zc = z * 2 + c
    stats_a[me_xy] = jnp.zeros((NZ, STAT), jnp.float32)

    def compute(s):
        zx = plane(s)
        left = held[0, zx].reshape(BLOCK, HALF)
        total = lax.dot_general(head_ref[:, :HALF], left, (((1,), (1,)), ((), ())), preferred_element_type=jnp.float32)
        right = jnp.concatenate([held[1, zx, yy, xx] for xx in range(NX) for yy in range(NY)], axis=0)
        total += lax.dot_general(head_ref[:, HALF:], right, (((1,), (1,)), ((), ())), preferred_element_type=jnp.float32)
        logits[zx] = total
        highest = jnp.max(total, axis=0, keepdims=True)
        lse = highest + jnp.log(jnp.sum(jnp.exp(total - highest), axis=0, keepdims=True))
        labels = true_ref[pl.ds(zx, 1), :]
        picked = jnp.sum(jnp.where(rows == labels, total, 0.0), axis=0, keepdims=True)
        fresh_row = jnp.concatenate([lse, picked[:, :128] + picked[:, 128:]], axis=1)
        stats_a[me_xy] = jnp.where(planes == zx, fresh_row, stats_a[me_xy])

    def step(i, carry):
        @pl.when(jnp.logical_or(i == 1, i == 2))
        def _():
            for r in range(4):
                piece = slab(q)
                remote(piece, piece, zf_s.at[i - 1, r], zf_r.at[i - 1, r], sister).wait_recv()

        @pl.when(jnp.logical_and(i >= 3, i <= 6))
        def _():
            z_copy(i - 2).wait_recv()

        @pl.when(jnp.logical_and(i >= 1, i <= 4))
        def _():
            z_copy(i).start()

        @pl.when(jnp.logical_or(i == 5, i == 6))
        def _():
            z_half(i).start()

        @pl.when(i == 7)
        def _():
            z_half(5).wait_recv()
            z_half(6).wait_recv()

        @pl.when(jnp.logical_and(i >= 1, i <= 7))
        def _():
            for copy in p_copies(i):
                copy.start()
            s_copy(i, 0, p).start()

        @pl.when(jnp.logical_and(i >= LAG1, i <= LAG1 + 7))
        def _():
            s = i - LAG1
            on, back = p_halves(s)

            def arrived(way):
                @pl.when(s == 0)
                def _():
                    for r in range(4):
                        piece = slab(q)
                        remote(piece, piece, pf_s.at[way, r], pf_r.at[way, r], sister).wait_recv()

                @pl.when(s > 0)
                def _():
                    p_copies(s)[way].wait_recv()

            arrived(0)
            on.start()
            s_copy(s, 1, p_dn).start()
            arrived(1)
            back.start()
            s_copy(s, 2, p_up).start()

        @pl.when(jnp.logical_and(i >= LAG2, i <= LAG2 + 7))
        def _():
            s = i - LAG2
            on, back = p_halves(s)
            on.wait_recv()
            back.wait_recv()
            s_copy(s, 3, p_far).start()

        @pl.when(i >= LAG3)
        def _():
            s = i - LAG3
            for which in range(4):
                s_copy(s, which, p).wait_recv()
            compute(s)

        return carry

    head_copy.wait()
    lax.fori_loop(1, 8 + LAG3, step, 0)

    def a_copy(j):
        return remote(stats_a.at[me_xy], stats_a.at[me_xy], a_s.at[j], a_r.at[me_xy], (j // 4, (j % 4) * 16 + z * 2 + c))

    def a_arrival(j):
        return remote(stats_a.at[j], stats_a.at[j], a_s.at[j], a_r.at[j], (j // 4, (j % 4) * 16 + z * 2 + c))

    def b_copy(j):
        return remote(stats_b.at[me_zc], stats_b.at[me_zc], b_s.at[j], b_r.at[me_zc], (x, y * 16 + j))

    def b_arrival(j):
        return remote(stats_b.at[j], stats_b.at[j], b_s.at[j], b_r.at[j], (x, y * 16 + j))

    def each_other(me, action):
        def one(j, carry):
            @pl.when(j != me)
            def _():
                action(j)
            return carry
        lax.fori_loop(0, 16, one, 0)

    def combine(stats):
        values = [stats[j] for j in range(16)]
        top = values[0]
        for value in values[1:]:
            top = jnp.maximum(top, value)
        total = jnp.exp(values[0] - top)
        added = values[0]
        for value in values[1:]:
            total += jnp.exp(value - top)
            added += value
        return jnp.where(lanes < BLOCK, top + jnp.log(total), added)

    each_other(me_xy, lambda j: a_copy(j).start())

    pair_copy.wait_send()
    for copy in q_copies:
        copy.wait_send()
    for r in range(4):
        for copy in early(r):
            copy.wait_send()

    def finish(s, carry):
        @pl.when(jnp.logical_and(s >= 1, s <= 4))
        def _():
            z_copy(s).wait_send()

        @pl.when(s >= 1)
        def _():
            for copy in p_copies(s):
                copy.wait_send()

        for copy in p_halves(s):
            copy.wait_send()
        for which in range(4):
            s_copy(s, which, p).wait_send()
        return carry

    lax.fori_loop(0, 8, finish, 0)
    z_half(5).wait_send()
    z_half(6).wait_send()

    each_other(me_xy, lambda j: a_arrival(j).wait_recv())
    stats_b[me_zc] = combine(stats_a)
    each_other(me_zc, lambda j: b_copy(j).start())
    each_other(me_xy, lambda j: a_copy(j).wait_send())
    each_other(me_zc, lambda j: b_arrival(j).wait_recv())
    final = combine(stats_b)
    signed = jnp.where(lanes < BLOCK, final, -final)
    loss_ref[...] = jnp.sum(jnp.sum(signed, axis=1, keepdims=True), axis=0, keepdims=True) * (1.0 / TOKENS)
    for zx in range(NZ):
        log_norm = final[zx:zx + 1, :BLOCK]
        chosen = (rows == samp_ref[zx:zx + 1, :]).astype(jnp.float32)
        signal_ref[:, zx * BLOCK:(zx + 1) * BLOCK] = (jnp.exp(logits[zx] - log_norm) - chosen).astype(jnp.bfloat16)
    each_other(me_zc, lambda j: b_copy(j).wait_send())


def gather_call(features, head, true_labels, sampled_labels):
    dma = pltpu.SemaphoreType.DMA
    vmem = pl.BlockSpec(memory_space=pltpu.VMEM)
    hbm = pl.BlockSpec(memory_space=pltpu.HBM)
    return pl.pallas_call(
        gather_kernel,
        out_shape=(
            jax.ShapeDtypeStruct((2, NZ, 4, 4, ROWS, HALF), jnp.bfloat16),
            jax.ShapeDtypeStruct((VOC, TOKENS), jnp.bfloat16),
            jax.ShapeDtypeStruct((1, 1), jnp.float32),
        ),
        in_specs=[hbm] * 4,
        out_specs=(vmem, vmem, vmem),
        scratch_shapes=[
            pltpu.VMEM((2, 8, HALF), jnp.bfloat16),
            pltpu.VMEM((VOC, D), jnp.bfloat16),
            pltpu.VMEM((2, 16, 128), jnp.int32),
            pltpu.VMEM((NZ, BLOCK), jnp.int32),
            pltpu.VMEM((NZ, BLOCK), jnp.int32),
            pltpu.VMEM((NZ, VOC, BLOCK), jnp.float32),
            pltpu.VMEM((16, NZ, STAT), jnp.float32),
            pltpu.VMEM((16, NZ, STAT), jnp.float32),
            dma, dma, dma((3,)), dma((3,)), dma((2, 4)), dma((2, 4)), dma((8,)), dma((8,)), dma((2,)), dma((2,)),
            dma((2, 4)), dma((2, 4)), dma((8, 4)), dma((8, 4)), dma((8, 4)), dma((8, 4)),
            dma((16,)), dma((16,)), dma((16,)), dma((16,)), dma, dma, dma((2,)),
        ],
        compiler_params=pltpu.CompilerParams(collective_id=0, has_side_effects=True, vmem_limit_bytes=20 << 20),
        name="gather_logits",
    )(features, head, true_labels, sampled_labels)


def update_kernel(signal_ref, feats_ref, momentum_ref, hessian_ref, fresh_ref, clipped_ref):
    j = pl.program_id(0)
    width = fresh_ref.shape[1]
    steps = HALF // width

    def update(half):
        columns = pl.ds(pl.multiple_of((j - half * steps) * width, width), width)
        if half == 0:
            feats = feats_ref[0, :, :, :, :, columns].reshape(TOKENS, width)
        else:
            feats = jnp.concatenate(
                [feats_ref[1, zz, yy, xx, :, columns] for zz in range(NZ) for xx in range(NX) for yy in range(NY)], axis=0)
        gradient = jnp.dot(signal_ref[...], feats, preferred_element_type=jnp.float32)
        fresh = hess_decay * hessian_ref[...].astype(jnp.float32) + (1.0 - hess_decay) * gradient * gradient
        fresh_ref[...] = fresh.astype(jnp.bfloat16)
        clipped = jnp.clip(momentum_ref[...].astype(jnp.float32) / (clip_scale * fresh), -1.0, 1.0)
        clipped_ref[...] = clipped.astype(jnp.bfloat16)

    pl.when(j < steps)(lambda: update(0))
    pl.when(j >= steps)(lambda: update(1))


def update_call(signal, feats, momentum, hessian):
    width = 1024
    tile = pl.BlockSpec((VOC, width), lambda j: (0, j))
    out = jax.ShapeDtypeStruct((VOC, D), jnp.bfloat16)
    return pl.pallas_call(
        update_kernel,
        grid=(D // width,),
        out_shape=(out, out),
        in_specs=[
            pl.BlockSpec(memory_space=pltpu.VMEM),
            pl.BlockSpec(memory_space=pltpu.VMEM),
            tile,
            tile,
        ],
        out_specs=(tile, tile),
        compiler_params=pltpu.CompilerParams(vmem_limit_bytes=20 << 20),
        name="gradient_update",
    )(signal, feats, momentum, hessian)


def shards(features, head, momentum, hessian, true_labels, sampled_labels):
    features, head, momentum, hessian, true_labels, sampled_labels = (
        pltpu.with_memory_space_constraint(a, pltpu.HBM)
        for a in (features, head, momentum, hessian, true_labels.reshape(16, 128), sampled_labels.reshape(16, 128)))
    feats, signal, loss = gather_call(features, head, true_labels, sampled_labels)
    fresh, clipped = update_call(signal, feats, momentum, hessian)
    return (loss.reshape(()), fresh, clipped)


def solution(mesh):
    rows = P(("dp", "vocab"), None)
    return jax.shard_map(
        shards,
        mesh=mesh,
        in_specs=(rows, rows, rows, rows, P(), P()),
        out_specs=(P(), rows, rows),
        check_vma=False,
    )
```

time: 97.5 us -> 83.2 us (0.85)
  Pallas kernels: 88.7 us -> 80.6 us
  local copies, waits for them, and re-layouts: 5.83 us -> 0 us
    pallas_call x1, Pallas kernels: 12.4 us -> 8.27 us  [update_call(): pl.pallas_call(update_kernel, grid=(D // width,), out_shape=(out, out), i...]
    unnamed x8 -> x0, local copies, waits for them, and re-layouts: 4.02 us -> none
    pallas_call x1, Pallas kernels: 76.3 us -> 72.3 us  [gather_call(): pl.pallas_call(gather_kernel, out_shape=(jax.ShapeDtypeStruct((2, NZ, 4,...]
    reshape x4 -> x0, local copies, waits for them, and re-layouts: 1.77 us -> none  [by_plane(): labels.reshape(NX, NY, NZ, ROWS).transpose(2, 0, 1, 3).reshape(NZ, BLOCK)]
where the time goes in v2:
time: 83.2 us; the launch traced here: 83 us
  Pallas kernels  80.6 us (97%)
  between operations  2.4 us (3%)
    pallas_call x1, Pallas kernels, gather_call(): pl.pallas_call(gather_kernel, out_shape=(jax.ShapeDtypeStruct((2, NZ, 4,...  72.3 us
    pallas_call x1, Pallas kernels, update_call(): pl.pallas_call(update_kernel, grid=(D // width,), out_shape=(out, out), i...  8.27 us

profile of v2, /device:TPU:1, one launch (start us, length us, event | category | flops | bytes accessed | tf_op | source)
XLA Modules:
  0.0 83.0 jit_solution(167987557921968144)
XLA Ops:
  0.6 72.3 %gather_logits.1 = (bf16[2,8,4,4,16,2048]{5,4,3,2,1,0:T(8,128)(2,1)S(1)}, bf16[256,2048]{1,0:T(8,128)(2,1)S(1)}, f32[1,1]{1,0:T(1,128)}) custom-call(bf16[8,4096]{1,0:T(8,128)(2,1)} %feat_ref.1, bf16[256,4096]{1,0:T(8,128)(2,1)} %head_hbm.1, s32[16,128]{1,0:T(8,128)} %bitcast.3, s32[16,128]{1,0:T(8,128)} %bitcast.4), custom_call_target="tpu_custom_call" | custom-call | tf_op jit(solution)/shard_map/gather_logits/pallas_call | solution.py:328
  72.9 8.3 %gradient_update.1 = (bf16[256,4096]{1,0:T(8,128)(2,1)}, bf16[256,4096]{1,0:T(8,128)(2,1)}) custom-call(bf16[256,2048]{1,0:T(8,128)(2,1)S(1)} %get-tuple-element.9.signal_ref, bf16[2,8,4,4,16,2048]{5,4,3,2,1,0:T(8,128)(2,1)S(1)} %get-tuple-element.10.feats_ref, bf16[256,4096]{1,0:T(8,128)(2,1)} %momentum_ref.1, bf16[256,4096]{1,0:T(8,128)(2,1)} %hessian_ref.1), custom_call_target="tpu_custom_call" | custom-call | tf_op jit(solution)/shard_map/gradient_update/pallas_call | solution.py:381

commit v3 on v2

--- a/solution.py
+++ b/solution.py
@@ -17,7 +17,7 @@
 TOKENS = 2048
 VOC = 256
 STAT = 384
-LAG1, LAG2, LAG3 = 2, 4, 5
+LAG1, LAG2, LAG3 = 6, 12, 14
 
 
 def permute_labels(raw_ref, true_ref, samp_ref):
@@ -35,11 +35,11 @@
         samp_ref[zx:zx + 1, :] = (rows[1] * 256.0 + rows[3]).astype(jnp.int32)
 
 
-def gather_kernel(feat_ref, head_hbm, true_hbm, samp_hbm,
-                  held, signal_ref, loss_ref,
+def gather_kernel(feat_ref, head_hbm, momentum_hbm, hessian_hbm, true_hbm, samp_hbm,
+                  held, signal_ref, momentum_ref, hessian_ref, loss_ref,
                   pair, head_ref, raw_ref, true_ref, samp_ref, logits, stats_a, stats_b,
-                  pair_s, pair_r, q_s, q_r, zf_s, zf_r, z_s, z_r, zh_s, zh_r,
-                  pf_s, pf_r, p_s, p_r, s_s, s_r, a_s, a_r, b_s, b_r, own_sem, head_sem, raw_sem):
+                  pair_s, pair_r, q_s, q_r, zf_s, zf_r, z_s, z_r,
+                  pf_s, pf_r, p_s, p_r, far_s, far_r, s_s, s_r, a_s, a_r, b_s, b_r, own_sem, head_sem, raw_sem, state_sem):
     x = lax.axis_index("dp")
     v = lax.axis_index("vocab")
     y, z, c = v // 16, (v // 2) % 8, v % 2
@@ -68,10 +68,10 @@
     own_copy = pltpu.make_async_copy(feat_ref.at[:, pl.ds(pl.multiple_of(c * HALF, HALF), HALF)], pair.at[c], own_sem)
     own_copy.start()
     barrier = pltpu.get_barrier_semaphore()
-    for dev in (sister, device(p_up, q, z), device(p_dn, q, z), device(p, q_up, z), device(p, q_dn, z),
+    for dev in (sister, device(p_up, q, z), device(p_dn, q, z), device(p, q_up, z), device(p, q_dn, z), device(p, q_far, z),
                 device(p, q, z_up), device(p, q, z_dn)):
         pl.semaphore_signal(barrier, inc=1, device_id=dev, device_id_type=MESH)
-    pl.semaphore_wait(barrier, 7)
+    pl.semaphore_wait(barrier, 8)
 
     theirs = pl.multiple_of((1 - c) * HALF, HALF)
     pair_copy = remote(feat_ref.at[:, pl.ds(theirs, HALF)], pair.at[c], pair_s, pair_r, sister)
@@ -83,11 +83,8 @@
     def slab(qx):
         return held.at[c, z, p, qx]
 
-    q_copies = [
-        remote(slab(q), slab(q), q_s.at[0], q_r.at[0], device(p, q_up, z)),
-        remote(slab(q), slab(q), q_s.at[1], q_r.at[1], device(p, q_dn, z)),
-        remote(slab(q_dn), slab(q_dn), q_s.at[2], q_r.at[2], device(p, q_up, z)),
-    ]
+    own = slab(q)
+    q_copies = [remote(own, own, q_s.at[k], q_r.at[k], device(p, to, z)) for k, to in enumerate((q_up, q_dn, q_far))]
     order = (q, q_dn, q_up, q_far)
 
     def early(r):
@@ -111,44 +108,40 @@
     def part(zx, px, half):
         return held.at[c, zx, px, pl.ds(half * 2, 2)]
 
-    def z_copy(s):
-        zx = plane(s)
+    def z_copy(s, h):
+        piece = part(plane(s), p, h)
         to = jnp.where(s % 2 == 1, z_up, z_dn)
-        return remote(chunk(zx, p), chunk(zx, p), z_s.at[s + 2], z_r.at[s + 2], device(p, q, to))
-
-    def z_half(s):
-        zx = plane(s)
-        to = jnp.where(s % 2 == 1, z_up, z_dn)
-        return remote(part(zx, p, s - 5), part(zx, p, s - 5), zh_s.at[s - 5], zh_r.at[s - 5], device(p, q, to))
-
-    def p_copies(s):
-        zx = plane(s)
-        return (remote(chunk(zx, p), chunk(zx, p), p_s.at[s, 0], p_r.at[s, 0], device(p_up, q, z)),
-                remote(chunk(zx, p), chunk(zx, p), p_s.at[s, 1], p_r.at[s, 1], device(p_dn, q, z)))
-
-    def p_halves(s):
-        zx = plane(s)
-        return (remote(part(zx, p_dn, 0), part(zx, p_dn, 0), p_s.at[s, 2], p_r.at[s, 2], device(p_up, q, z)),
-                remote(part(zx, p_up, 1), part(zx, p_up, 1), p_s.at[s, 3], p_r.at[s, 3], device(p_dn, q, z)))
+        later = jnp.minimum(s + 2, 7)
+        return remote(piece, piece, z_s.at[later, h], z_r.at[later, h], device(p, q, to))
+
+    def p_copies(s, h):
+        piece = part(plane(s), p, h)
+        return (remote(piece, piece, p_s.at[s, 0, h], p_r.at[s, 0, h], device(p_up, q, z)),
+                remote(piece, piece, p_s.at[s, 1, h], p_r.at[s, 1, h], device(p_dn, q, z)))
+
+    def far_copy(s, h):
+        piece = part(plane(s), jnp.where(h == 0, p_dn, p_up), h)
+        return remote(piece, piece, far_s.at[s, h], far_r.at[s, h], device(jnp.where(h == 0, p_up, p_dn), q, z))
 
     def s_copy(s, which, px):
-        zx = plane(s)
-        return remote(chunk(zx, px), chunk(zx, px), s_s.at[s, which], s_r.at[s, which], sister)
-
-    q_copies[0].start()
-    q_copies[1].start()
+        piece = chunk(plane(s), px)
+        return remote(piece, piece, s_s.at[s, which], s_r.at[s, which], sister)
+
+    for copy in q_copies:
+        copy.start()
     start_early(0)
-    q_copies[0].wait_recv()
-    q_copies[2].start()
-    start_early(1)
-    q_copies[1].wait_recv()
-    start_early(2)
+    for r in range(1, 4):
+        q_copies[r - 1].wait_recv()
+        start_early(r)
+    s_copy(0, 0, p).start()
     for copy in raw_copies:
         copy.wait()
     permute_labels(raw_ref, true_ref, samp_ref)
-    q_copies[2].wait_recv()
-    start_early(3)
-    s_copy(0, 0, p).start()
+
+    state_copies = [pltpu.make_async_copy(momentum_hbm, momentum_ref, state_sem.at[0]),
+                    pltpu.make_async_copy(hessian_hbm, hessian_ref, state_sem.at[1])]
+    for copy in state_copies:
+        copy.start()
 
     own_offset = (x * 64 + v) * VOC
     rows = own_offset + lax.broadcasted_iota(jnp.int32, (VOC, BLOCK), 0)
@@ -172,70 +165,68 @@
         fresh_row = jnp.concatenate([lse, picked[:, :128] + picked[:, 128:]], axis=1)
         stats_a[me_xy] = jnp.where(planes == zx, fresh_row, stats_a[me_xy])
 
-    def step(i, carry):
-        @pl.when(jnp.logical_or(i == 1, i == 2))
+    def step(u, carry):
+        @pl.when(jnp.logical_and(u >= LAG1, u <= LAG1 + 15))
         def _():
-            for r in range(4):
-                piece = slab(q)
-                remote(piece, piece, zf_s.at[i - 1, r], zf_r.at[i - 1, r], sister).wait_recv()
-
-        @pl.when(jnp.logical_and(i >= 3, i <= 6))
-        def _():
-            z_copy(i - 2).wait_recv()
-
-        @pl.when(jnp.logical_and(i >= 1, i <= 4))
-        def _():
-            z_copy(i).start()
-
-        @pl.when(jnp.logical_or(i == 5, i == 6))
-        def _():
-            z_half(i).start()
-
-        @pl.when(i == 7)
-        def _():
-            z_half(5).wait_recv()
-            z_half(6).wait_recv()
-
-        @pl.when(jnp.logical_and(i >= 1, i <= 7))
-        def _():
-            for copy in p_copies(i):
-                copy.start()
-            s_copy(i, 0, p).start()
-
-        @pl.when(jnp.logical_and(i >= LAG1, i <= LAG1 + 7))
-        def _():
-            s = i - LAG1
-            on, back = p_halves(s)
-
-            def arrived(way):
-                @pl.when(s == 0)
-                def _():
+            s, h = (u - LAG1) // 2, (u - LAG1) % 2
+
+            @pl.when(jnp.logical_and(s == 0, h == 0))
+            def _():
+                for way in range(2):
                     for r in range(4):
                         piece = slab(q)
                         remote(piece, piece, pf_s.at[way, r], pf_r.at[way, r], sister).wait_recv()
 
-                @pl.when(s > 0)
-                def _():
-                    p_copies(s)[way].wait_recv()
-
-            arrived(0)
-            on.start()
-            s_copy(s, 1, p_dn).start()
-            arrived(1)
-            back.start()
-            s_copy(s, 2, p_up).start()
-
-        @pl.when(jnp.logical_and(i >= LAG2, i <= LAG2 + 7))
+            @pl.when(s > 0)
+            def _():
+                for copy in p_copies(s, h):
+                    copy.wait_recv()
+
+            far_copy(s, h).start()
+
+            @pl.when(h == 1)
+            def _():
+                s_copy(s, 1, p_dn).start()
+                s_copy(s, 2, p_up).start()
+
+        @pl.when(u <= 15)
         def _():
-            s = i - LAG2
-            on, back = p_halves(s)
-            on.wait_recv()
-            back.wait_recv()
-            s_copy(s, 3, p_far).start()
-
-        @pl.when(i >= LAG3)
+            s, h = u // 2, u % 2
+
+            @pl.when(jnp.logical_and(s <= 2, h == 0))
+            def _():
+                for r in range(4):
+                    piece = slab(q)
+                    remote(piece, piece, zf_s.at[s - 1, r], zf_r.at[s - 1, r], sister).wait_recv()
+
+            @pl.when(s >= 3)
+            def _():
+                piece = part(plane(s), p, h)
+                remote(piece, piece, z_s.at[s, h], z_r.at[s, h], sister).wait_recv()
+
+            @pl.when(jnp.logical_or(s <= 4, s == 5 + h))
+            def _():
+                z_copy(s, h).start()
+
+            for copy in p_copies(s, h):
+                copy.start()
+
+            @pl.when(h == 1)
+            def _():
+                s_copy(s, 0, p).start()
+
+        @pl.when(jnp.logical_and(u >= LAG2, u <= LAG2 + 15))
         def _():
-            s = i - LAG3
+            s, h = (u - LAG2) // 2, (u - LAG2) % 2
+            far_copy(s, h).wait_recv()
+
+            @pl.when(h == 1)
+            def _():
+                s_copy(s, 3, p_far).start()
+
+        @pl.when(jnp.logical_and(u >= LAG3, (u - LAG3) % 2 == 1))
+        def _():
+            s = (u - LAG3) // 2
             for which in range(4):
                 s_copy(s, which, p).wait_recv()
             compute(s)
@@ -243,7 +234,7 @@
         return carry
 
     head_copy.wait()
-    lax.fori_loop(1, 8 + LAG3, step, 0)
+    lax.fori_loop(2, 16 + LAG3, step, 0)
 
     def a_copy(j):
         return remote(stats_a.at[me_xy], stats_a.at[me_xy], a_s.at[j], a_r.at[me_xy], (j // 4, (j % 4) * 16 + z * 2 + c))
@@ -264,6 +255,12 @@
                 action(j)
             return carry
         lax.fori_loop(0, 16, one, 0)
+
+    def span(n, k):
+        return min(k, n - k)
+
+    xy_order = sorted(((i, k) for i in range(NX) for k in range(NY) if i or k), key=lambda o: -span(NX, o[0]) - span(NY, o[1]))
+    zc_order = sorted(((i, k) for i in range(NZ) for k in range(2) if i or k), key=lambda o: -span(NZ, o[0]) * 2 - o[1])
 
     def combine(stats):
         values = [stats[j] for j in range(16)]
@@ -277,7 +274,8 @@
             added += value
         return jnp.where(lanes < BLOCK, top + jnp.log(total), added)
 
-    each_other(me_xy, lambda j: a_copy(j).start())
+    for dx, dy in xy_order:
+        a_copy(((x + dx) % NX) * 4 + (y + dy) % NY).start()
 
     pair_copy.wait_send()
     for copy in q_copies:
@@ -287,30 +285,33 @@
             copy.wait_send()
 
     def finish(s, carry):
-        @pl.when(jnp.logical_and(s >= 1, s <= 4))
-        def _():
-            z_copy(s).wait_send()
-
-        @pl.when(s >= 1)
-        def _():
-            for copy in p_copies(s):
-                copy.wait_send()
-
-        for copy in p_halves(s):
-            copy.wait_send()
+        for h in range(2):
+            @pl.when(jnp.logical_and(s >= 1, jnp.logical_or(s <= 4, s == 5 + h)))
+            def _():
+                z_copy(s, h).wait_send()
+
+            @pl.when(s >= 1)
+            def _():
+                for copy in p_copies(s, h):
+                    copy.wait_send()
+
+            far_copy(s, h).wait_send()
         for which in range(4):
             s_copy(s, which, p).wait_send()
         return carry
 
     lax.fori_loop(0, 8, finish, 0)
-    z_half(5).wait_send()
-    z_half(6).wait_send()
-
-    each_other(me_xy, lambda j: a_arrival(j).wait_recv())
+    for copy in state_copies:
+        copy.wait()
+
+    for dx, dy in reversed(xy_order):
+        a_arrival(((x + dx) % NX) * 4 + (y + dy) % NY).wait_recv()
     stats_b[me_zc] = combine(stats_a)
-    each_other(me_zc, lambda j: b_copy(j).start())
+    for dz, dc in zc_order:
+        b_copy(((z + dz) % NZ) * 2 + (c + dc) % 2).start()
     each_other(me_xy, lambda j: a_copy(j).wait_send())
-    each_other(me_zc, lambda j: b_arrival(j).wait_recv())
+    for dz, dc in reversed(zc_order):
+        b_arrival(((z + dz) % NZ) * 2 + (c + dc) % 2).wait_recv()
     final = combine(stats_b)
     signed = jnp.where(lanes < BLOCK, final, -final)
     loss_ref[...] = jnp.sum(jnp.sum(signed, axis=1, keepdims=True), axis=0, keepdims=True) * (1.0 / TOKENS)
@@ -321,7 +322,7 @@
     each_other(me_zc, lambda j: b_copy(j).wait_send())
 
 
-def gather_call(features, head, true_labels, sampled_labels):
+def gather_call(features, head, momentum, hessian, true_labels, sampled_labels):
     dma = pltpu.SemaphoreType.DMA
     vmem = pl.BlockSpec(memory_space=pltpu.VMEM)
     hbm = pl.BlockSpec(memory_space=pltpu.HBM)
@@ -330,10 +331,12 @@
         out_shape=(
             jax.ShapeDtypeStruct((2, NZ, 4, 4, ROWS, HALF), jnp.bfloat16),
             jax.ShapeDtypeStruct((VOC, TOKENS), jnp.bfloat16),
+            jax.ShapeDtypeStruct((VOC, D), jnp.bfloat16),
+            jax.ShapeDtypeStruct((VOC, D), jnp.bfloat16),
             jax.ShapeDtypeStruct((1, 1), jnp.float32),
         ),
-        in_specs=[hbm] * 4,
-        out_specs=(vmem, vmem, vmem),
+        in_specs=[hbm] * 6,
+        out_specs=(vmem,) * 5,
         scratch_shapes=[
             pltpu.VMEM((2, 8, HALF), jnp.bfloat16),
             pltpu.VMEM((VOC, D), jnp.bfloat16),
@@ -343,13 +346,13 @@
             pltpu.VMEM((NZ, VOC, BLOCK), jnp.float32),
             pltpu.VMEM((16, NZ, STAT), jnp.float32),
             pltpu.VMEM((16, NZ, STAT), jnp.float32),
-            dma, dma, dma((3,)), dma((3,)), dma((2, 4)), dma((2, 4)), dma((8,)), dma((8,)), dma((2,)), dma((2,)),
-            dma((2, 4)), dma((2, 4)), dma((8, 4)), dma((8, 4)), dma((8, 4)), dma((8, 4)),
-            dma((16,)), dma((16,)), dma((16,)), dma((16,)), dma, dma, dma((2,)),
+            dma, dma, dma((3,)), dma((3,)), dma((2, 4)), dma((2, 4)), dma((8, 2)), dma((8, 2)),
+            dma((2, 4)), dma((2, 4)), dma((8, 2, 2)), dma((8, 2, 2)), dma((8, 2)), dma((8, 2)), dma((8, 4)), dma((8, 4)),
+            dma((16,)), dma((16,)), dma((16,)), dma((16,)), dma, dma, dma((2,)), dma((2,)),
         ],
         compiler_params=pltpu.CompilerParams(collective_id=0, has_side_effects=True, vmem_limit_bytes=20 << 20),
         name="gather_logits",
-    )(features, head, true_labels, sampled_labels)
+    )(features, head, momentum, hessian, true_labels, sampled_labels)
 
 
 def update_kernel(signal_ref, feats_ref, momentum_ref, hessian_ref, fresh_ref, clipped_ref):
@@ -359,15 +362,16 @@
 
     def update(half):
         columns = pl.ds(pl.multiple_of((j - half * steps) * width, width), width)
+        whole = pl.ds(pl.multiple_of(j * width, width), width)
         if half == 0:
             feats = feats_ref[0, :, :, :, :, columns].reshape(TOKENS, width)
         else:
             feats = jnp.concatenate(
                 [feats_ref[1, zz, yy, xx, :, columns] for zz in range(NZ) for xx in range(NX) for yy in range(NY)], axis=0)
         gradient = jnp.dot(signal_ref[...], feats, preferred_element_type=jnp.float32)
-        fresh = hess_decay * hessian_ref[...].astype(jnp.float32) + (1.0 - hess_decay) * gradient * gradient
+        fresh = hess_decay * hessian_ref[:, whole].astype(jnp.float32) + (1.0 - hess_decay) * gradient * gradient
         fresh_ref[...] = fresh.astype(jnp.bfloat16)
-        clipped = jnp.clip(momentum_ref[...].astype(jnp.float32) / (clip_scale * fresh), -1.0, 1.0)
+        clipped = jnp.clip(momentum_ref[:, whole].astype(jnp.float32) / (clip_scale * fresh), -1.0, 1.0)
         clipped_ref[...] = clipped.astype(jnp.bfloat16)
 
     pl.when(j < steps)(lambda: update(0))
@@ -385,8 +389,8 @@
         in_specs=[
             pl.BlockSpec(memory_space=pltpu.VMEM),
             pl.BlockSpec(memory_space=pltpu.VMEM),
-            tile,
-            tile,
+            pl.BlockSpec(memory_space=pltpu.VMEM),
+            pl.BlockSpec(memory_space=pltpu.VMEM),
         ],
         out_specs=(tile, tile),
         compiler_params=pltpu.CompilerParams(vmem_limit_bytes=20 << 20),
@@ -398,7 +402,7 @@
     features, head, momentum, hessian, true_labels, sampled_labels = (
         pltpu.with_memory_space_constraint(a, pltpu.HBM)
         for a in (features, head, momentum, hessian, true_labels.reshape(16, 128), sampled_labels.reshape(16, 128)))
-    feats, signal, loss = gather_call(features, head, true_labels, sampled_labels)
+    feats, signal, momentum, hessian, loss = gather_call(features, head, momentum, hessian, true_labels, sampled_labels)
     fresh, clipped = update_call(signal, feats, momentum, hessian)
     return (loss.reshape(()), fresh, clipped)
 

time: 83.2 us -> 82.1 us (0.987)
  Pallas kernels: 80.6 us -> 79.6 us
    pallas_call x1, Pallas kernels: 8.27 us -> 6.99 us  [update_call(): pl.pallas_call(update_kernel, grid=(D // width,), out_shape=(out, out), i...]
where the time goes in v3:
time: 82.1 us; the launch traced here: 82 us
  Pallas kernels  79.6 us (97%)
  between operations  2.4 us (3%)
    pallas_call x1, Pallas kernels, gather_call(): pl.pallas_call(gather_kernel, out_shape=(jax.ShapeDtypeStruct((2, NZ, 4,...  72.6 us
    pallas_call x1, Pallas kernels, update_call(): pl.pallas_call(update_kernel, grid=(D // width,), out_shape=(out, out), i...  6.99 us

profile of v3, /device:TPU:1, one launch (start us, length us, event | category | flops | bytes accessed | tf_op | source)
XLA Modules:
  0.0 82.0 jit_solution(6485364488360867790)
XLA Ops:
  0.6 72.6 %gather_logits.1 = (bf16[2,8,4,4,16,2048]{5,4,3,2,1,0:T(8,128)(2,1)S(1)}, bf16[256,2048]{1,0:T(8,128)(2,1)S(1)}, bf16[256,4096]{1,0:T(8,128)(2,1)S(1)}, bf16[256,4096]{1,0:T(8,128)(2,1)S(1)}, f32[1,1]{1,0:T(1,128)}) custom-call(bf16[8,4096]{1,0:T(8,128)(2,1)} %feat_ref.1, bf16[256,4096]{1,0:T(8,128)(2,1)} %head_hbm.1, bf16[256,4096]{1,0:T(8,128)(2,1)} %momentum_hbm.1, ...), custom_call_target="tpu_custom_call" | custom-call | tf_op jit(solution)/shard_map/gather_logits/pallas_call | solution.py:329
  73.2 7.0 %gradient_update.1 = (bf16[256,4096]{1,0:T(8,128)(2,1)}, bf16[256,4096]{1,0:T(8,128)(2,1)}) custom-call(bf16[256,2048]{1,0:T(8,128)(2,1)S(1)} %get-tuple-element.11.signal_ref, bf16[2,8,4,4,16,2048]{5,4,3,2,1,0:T(8,128)(2,1)S(1)} %get-tuple-element.12.feats_ref, bf16[256,4096]{1,0:T(8,128)(2,1)S(1)} %get-tuple-element.13.momentum_ref, ...), custom_call_target="tpu_custom_call" | custom-call | tf_op jit(solution)/shard_map/gradient_update/pallas_call | solution.py:385

commit v4 on v3

--- a/solution.py
+++ b/solution.py
@@ -16,7 +16,6 @@
 BLOCK = 256
 TOKENS = 2048
 VOC = 256
-STAT = 384
 LAG1, LAG2, LAG3 = 6, 12, 14
 
 
@@ -37,9 +36,9 @@
 
 def gather_kernel(feat_ref, head_hbm, momentum_hbm, hessian_hbm, true_hbm, samp_hbm,
                   held, signal_ref, momentum_ref, hessian_ref, loss_ref,
-                  pair, head_ref, raw_ref, true_ref, samp_ref, logits, stats_a, stats_b,
+                  pair, head_ref, raw_ref, true_ref, samp_ref, logits, stats_a, stats_b, pick_a, pick_b,
                   pair_s, pair_r, q_s, q_r, zf_s, zf_r, z_s, z_r,
-                  pf_s, pf_r, p_s, p_r, far_s, far_r, s_s, s_r, a_s, a_r, b_s, b_r, own_sem, head_sem, raw_sem, state_sem):
+                  pf_s, pf_r, p_s, p_r, far_s, far_r, s_s, s_r, a_s, a_r, b_s, b_r, c_s, c_r, d_s, d_r, own_sem, head_sem, raw_sem, state_sem):
     x = lax.axis_index("dp")
     v = lax.axis_index("vocab")
     y, z, c = v // 16, (v // 2) % 8, v % 2
@@ -145,11 +144,11 @@
 
     own_offset = (x * 64 + v) * VOC
     rows = own_offset + lax.broadcasted_iota(jnp.int32, (VOC, BLOCK), 0)
-    lanes = lax.broadcasted_iota(jnp.int32, (1, STAT), 1)
-    planes = lax.broadcasted_iota(jnp.int32, (NZ, STAT), 0)
+    planes = lax.broadcasted_iota(jnp.int32, (NZ, BLOCK), 0)
     me_xy = x * 4 + y
     me_zc = z * 2 + c
-    stats_a[me_xy] = jnp.zeros((NZ, STAT), jnp.float32)
+    stats_a[x * 4 + y] = jnp.zeros((NZ, BLOCK), jnp.float32)
+    pick_a[x * 4 + y] = jnp.zeros((1, 128), jnp.float32)
 
     def compute(s):
         zx = plane(s)
@@ -162,8 +161,8 @@
         lse = highest + jnp.log(jnp.sum(jnp.exp(total - highest), axis=0, keepdims=True))
         labels = true_ref[pl.ds(zx, 1), :]
         picked = jnp.sum(jnp.where(rows == labels, total, 0.0), axis=0, keepdims=True)
-        fresh_row = jnp.concatenate([lse, picked[:, :128] + picked[:, 128:]], axis=1)
-        stats_a[me_xy] = jnp.where(planes == zx, fresh_row, stats_a[me_xy])
+        stats_a[me_xy] = jnp.where(planes == zx, lse, stats_a[me_xy])
+        pick_a[me_xy] = pick_a[me_xy] + picked[:, :128] + picked[:, 128:]
 
     def step(u, carry):
         @pl.when(jnp.logical_and(u >= LAG1, u <= LAG1 + 15))
@@ -239,6 +238,18 @@
     def a_copy(j):
         return remote(stats_a.at[me_xy], stats_a.at[me_xy], a_s.at[j], a_r.at[me_xy], (j // 4, (j % 4) * 16 + z * 2 + c))
 
+    def c_copy(j):
+        return remote(pick_a.at[me_xy], pick_a.at[me_xy], c_s.at[j], c_r.at[me_xy], (j // 4, (j % 4) * 16 + z * 2 + c))
+
+    def d_copy(j):
+        return remote(pick_b.at[me_zc], pick_b.at[me_zc], d_s.at[j], d_r.at[me_zc], (x, y * 16 + j))
+
+    def c_arrival(j):
+        return remote(pick_a.at[j], pick_a.at[j], c_s.at[j], c_r.at[j], (j // 4, (j % 4) * 16 + z * 2 + c))
+
+    def d_arrival(j):
+        return remote(pick_b.at[j], pick_b.at[j], d_s.at[j], d_r.at[j], (x, y * 16 + j))
+
     def a_arrival(j):
         return remote(stats_a.at[j], stats_a.at[j], a_s.at[j], a_r.at[j], (j // 4, (j % 4) * 16 + z * 2 + c))
 
@@ -268,14 +279,20 @@
         for value in values[1:]:
             top = jnp.maximum(top, value)
         total = jnp.exp(values[0] - top)
-        added = values[0]
         for value in values[1:]:
             total += jnp.exp(value - top)
-            added += value
-        return jnp.where(lanes < BLOCK, top + jnp.log(total), added)
+        return top + jnp.log(total)
+
+    def add(picks):
+        total = picks[0]
+        for j in range(1, 16):
+            total += picks[j]
+        return total
 
     for dx, dy in xy_order:
         a_copy(((x + dx) % NX) * 4 + (y + dy) % NY).start()
+    for dx, dy in xy_order:
+        c_copy(((x + dx) % NX) * 4 + (y + dy) % NY).start()
 
     pair_copy.wait_send()
     for copy in q_copies:
@@ -309,17 +326,26 @@
     stats_b[me_zc] = combine(stats_a)
     for dz, dc in zc_order:
         b_copy(((z + dz) % NZ) * 2 + (c + dc) % 2).start()
+    for dx, dy in reversed(xy_order):
+        c_arrival(((x + dx) % NX) * 4 + (y + dy) % NY).wait_recv()
+    pick_b[me_zc] = add(pick_a)
+    for dz, dc in zc_order:
+        d_copy(((z + dz) % NZ) * 2 + (c + dc) % 2).start()
     each_other(me_xy, lambda j: a_copy(j).wait_send())
     for dz, dc in reversed(zc_order):
         b_arrival(((z + dz) % NZ) * 2 + (c + dc) % 2).wait_recv()
     final = combine(stats_b)
-    signed = jnp.where(lanes < BLOCK, final, -final)
-    loss_ref[...] = jnp.sum(jnp.sum(signed, axis=1, keepdims=True), axis=0, keepdims=True) * (1.0 / TOKENS)
     for zx in range(NZ):
         log_norm = final[zx:zx + 1, :BLOCK]
         chosen = (rows == samp_ref[zx:zx + 1, :]).astype(jnp.float32)
         signal_ref[:, zx * BLOCK:(zx + 1) * BLOCK] = (jnp.exp(logits[zx] - log_norm) - chosen).astype(jnp.bfloat16)
+    for dz, dc in reversed(zc_order):
+        d_arrival(((z + dz) % NZ) * 2 + (c + dc) % 2).wait_recv()
+    spent = jnp.sum(jnp.sum(final, axis=1, keepdims=True), axis=0, keepdims=True)
+    loss_ref[...] = (spent - jnp.sum(add(pick_b), axis=1, keepdims=True)) * (1.0 / TOKENS)
     each_other(me_zc, lambda j: b_copy(j).wait_send())
+    each_other(me_xy, lambda j: c_copy(j).wait_send())
+    each_other(me_zc, lambda j: d_copy(j).wait_send())
 
 
 def gather_call(features, head, momentum, hessian, true_labels, sampled_labels):
@@ -344,11 +370,13 @@
             pltpu.VMEM((NZ, BLOCK), jnp.int32),
             pltpu.VMEM((NZ, BLOCK), jnp.int32),
             pltpu.VMEM((NZ, VOC, BLOCK), jnp.float32),
-            pltpu.VMEM((16, NZ, STAT), jnp.float32),
-            pltpu.VMEM((16, NZ, STAT), jnp.float32),
+            pltpu.VMEM((16, NZ, BLOCK), jnp.float32),
+            pltpu.VMEM((16, NZ, BLOCK), jnp.float32),
+            pltpu.VMEM((16, 1, 128), jnp.float32),
+            pltpu.VMEM((16, 1, 128), jnp.float32),
             dma, dma, dma((3,)), dma((3,)), dma((2, 4)), dma((2, 4)), dma((8, 2)), dma((8, 2)),
             dma((2, 4)), dma((2, 4)), dma((8, 2, 2)), dma((8, 2, 2)), dma((8, 2)), dma((8, 2)), dma((8, 4)), dma((8, 4)),
-            dma((16,)), dma((16,)), dma((16,)), dma((16,)), dma, dma, dma((2,)), dma((2,)),
+            *[dma((16,))] * 8, dma, dma, dma((2,)), dma((2,)),
         ],
         compiler_params=pltpu.CompilerParams(collective_id=0, has_side_effects=True, vmem_limit_bytes=20 << 20),
         name="gather_logits",

time: 82.1 us -> 81.6 us (level)
  no operation moved by 1% of the time
where the time goes in v4:
time: 81.6 us; the launch traced here: 81.5 us
  Pallas kernels  79.1 us (97%)
  between operations  2.4 us (3%)
    pallas_call x1, Pallas kernels, gather_call(): pl.pallas_call(gather_kernel, out_shape=(jax.ShapeDtypeStruct((2, NZ, 4,...  72.1 us
    pallas_call x1, Pallas kernels, update_call(): pl.pallas_call(update_kernel, grid=(D // width,), out_shape=(out, out), i...  7 us

profile of v4, /device:TPU:1, one launch (start us, length us, event | category | flops | bytes accessed | tf_op | source)
XLA Modules:
  0.0 81.5 jit_solution(11221943389461313498)
XLA Ops:
  0.6 72.1 %gather_logits.1 = (bf16[2,8,4,4,16,2048]{5,4,3,2,1,0:T(8,128)(2,1)S(1)}, bf16[256,2048]{1,0:T(8,128)(2,1)S(1)}, bf16[256,4096]{1,0:T(8,128)(2,1)S(1)}, bf16[256,4096]{1,0:T(8,128)(2,1)S(1)}, f32[1,1]{1,0:T(1,128)}) custom-call(bf16[8,4096]{1,0:T(8,128)(2,1)} %feat_ref.1, bf16[256,4096]{1,0:T(8,128)(2,1)} %head_hbm.1, bf16[256,4096]{1,0:T(8,128)(2,1)} %momentum_hbm.1, ...), custom_call_target="tpu_custom_call" | custom-call | tf_op jit(solution)/shard_map/gather_logits/pallas_call | solution.py:355
  72.7 7.0 %gradient_update.1 = (bf16[256,4096]{1,0:T(8,128)(2,1)}, bf16[256,4096]{1,0:T(8,128)(2,1)}) custom-call(bf16[256,2048]{1,0:T(8,128)(2,1)S(1)} %get-tuple-element.11.signal_ref, bf16[2,8,4,4,16,2048]{5,4,3,2,1,0:T(8,128)(2,1)S(1)} %get-tuple-element.12.feats_ref, bf16[256,4096]{1,0:T(8,128)(2,1)S(1)} %get-tuple-element.13.momentum_ref, ...), custom_call_target="tpu_custom_call" | custom-call | tf_op jit(solution)/shard_map/gradient_update/pallas_call | solution.py:413

commit v5 on v4

--- a/solution.py
+++ b/solution.py
@@ -407,7 +407,7 @@
 
 
 def update_call(signal, feats, momentum, hessian):
-    width = 1024
+    width = 2048
     tile = pl.BlockSpec((VOC, width), lambda j: (0, j))
     out = jax.ShapeDtypeStruct((VOC, D), jnp.bfloat16)
     return pl.pallas_call(

time: 81.6 us -> 81.6 us (level)
  no operation moved by 1% of the time
where the time goes in v5:
time: 81.6 us; the launch traced here: 81.5 us
  Pallas kernels  79 us (97%)
  between operations  2.4 us (3%)
    pallas_call x1, Pallas kernels, gather_call(): pl.pallas_call(gather_kernel, out_shape=(jax.ShapeDtypeStruct((2, NZ, 4,...  72.1 us
    pallas_call x1, Pallas kernels, update_call(): pl.pallas_call(update_kernel, grid=(D // width,), out_shape=(out, out), i...  6.98 us

profile of v5, /device:TPU:1, one launch (start us, length us, event | category | flops | bytes accessed | tf_op | source)
XLA Modules:
  0.0 81.5 jit_solution(4022182649454045624)
XLA Ops:
  0.6 72.1 %gather_logits.1 = (bf16[2,8,4,4,16,2048]{5,4,3,2,1,0:T(8,128)(2,1)S(1)}, bf16[256,2048]{1,0:T(8,128)(2,1)S(1)}, bf16[256,4096]{1,0:T(8,128)(2,1)S(1)}, bf16[256,4096]{1,0:T(8,128)(2,1)S(1)}, f32[1,1]{1,0:T(1,128)}) custom-call(bf16[8,4096]{1,0:T(8,128)(2,1)} %feat_ref.1, bf16[256,4096]{1,0:T(8,128)(2,1)} %head_hbm.1, bf16[256,4096]{1,0:T(8,128)(2,1)} %momentum_hbm.1, ...), custom_call_target="tpu_custom_call" | custom-call | tf_op jit(solution)/shard_map/gather_logits/pallas_call | solution.py:355
  72.7 7.0 %gradient_update.1 = (bf16[256,4096]{1,0:T(8,128)(2,1)}, bf16[256,4096]{1,0:T(8,128)(2,1)}) custom-call(bf16[256,2048]{1,0:T(8,128)(2,1)S(1)} %get-tuple-element.11.signal_ref, bf16[2,8,4,4,16,2048]{5,4,3,2,1,0:T(8,128)(2,1)S(1)} %get-tuple-element.12.feats_ref, bf16[256,4096]{1,0:T(8,128)(2,1)S(1)} %get-tuple-element.13.momentum_ref, ...), custom_call_target="tpu_custom_call" | custom-call | tf_op jit(solution)/shard_map/gradient_update/pallas_call | solution.py:413
